TPU v7x, 256 devices: a whole 4x4x8 slice. The times are simulated.
256 devices in a mesh: seq: 32 (over x_hi, z, core), batch: 8 (over x_lo, y).
Axes of the slice: x: 4 (x_hi: 2, x_lo: 2; x = x_hi * 2 + x_lo), y: 4, z: 8, core: 2. Of those that a mesh axis runs over, the one named last changes fastest.
Arguments:
- key_rows: bfloat16 [16384, 4096], P('seq', 'batch'), parts along dimension 1, may hold values from -6 to 6
- value_rows: bfloat16 [16384, 4096], P('seq', 'batch'), parts along dimension 1, may hold values from -6 to 6
- key_kernel: float32 [3, 4096], P(None, 'batch'), parts along dimension 1, may hold values from -3 to 3
- value_kernel: float32 [3, 4096], P(None, 'batch'), parts along dimension 1, may hold values from -3 to 3
- long_filter: bfloat16 [16384, 4096], P('seq', 'batch'), parts along dimension 1, may hold values from -0.046875 to 0.046875
- skip_gain: float32 [4096], P('batch'), parts along dimension 0, may hold values from 0.5 to 1.5
Outputs:
- filtered: bfloat16 [16384, 4096], P('seq', 'batch'), parts along dimension 1
There are 8 independent parts, one for each index of `batch`. A program takes and returns all parts, laid end to end along the dimension named above; each array names one. Nothing has to cross between parts.
All inputs are finite; a program needn't handle non-finite values.
Results may differ from a plain program's by a relative error of at most 0.011.
Values may be sent and summed in bfloat16 or wider, within the bound.
A program may use at most 64 MiB of HBM per device.

v0:
```python
import functools
import math

import jax
import jax.numpy as jnp
import numpy as np
from jax import lax
from jax.experimental import pallas as pl
from jax.experimental.pallas import tpu as pltpu
from jax.sharding import PartitionSpec as P

import ml_dtypes

MESH = pl.DeviceIdType.MESH
F32 = jnp.float32
BF16 = jnp.bfloat16
CHUNKS = 2
LANES = 8
HALVES = 2


def tables(n, rows):
    length = n * rows
    half = rows // HALVES
    outer = 2.0 * math.pi * np.outer(np.arange(n) + 0.25, np.arange(n)) / n
    pair = np.stack([np.cos(outer), -np.sin(outer)])
    first = np.einsum("pks,hg,cd->hpcksgd", pair, np.eye(HALVES), np.eye(LANES))
    first = first.reshape(HALVES, 2 * LANES * n, n * HALVES * LANES)
    last = first.reshape(-1, first.shape[-1]).T
    inner = 2.0 * math.pi * (np.outer(np.arange(rows), np.arange(rows)) % rows) / rows
    c, s = np.cos(inner), np.sin(inner)
    middle = np.block([[c, -s], [s, c]])
    twist = 2.0 * math.pi * np.outer(np.arange(n) + 0.25, np.arange(rows)) / length
    low = lambda a: np.ascontiguousarray(a).astype(ml_dtypes.bfloat16)
    return (
        low(first),
        low(last),
        low(middle),
        np.stack([np.cos(twist), np.sin(twist)]).astype(np.float32),
    )


def kernel(
    n,
    key_hbm,
    value_hbm,
    key_kernel,
    value_kernel,
    filter_hbm,
    skip,
    first_hbm,
    last_hbm,
    middle_hbm,
    twist_hbm,
    out_hbm,
    keys,
    values,
    filt,
    first,
    last,
    middle,
    twist,
    rim,
    send,
    recv,
    spectrum,
    mixed,
    stacked,
    out,
    in_sem,
    rim_send,
    rim_recv,
    send_sem,
    recv_sem,
    out_sem,
):
    me = lax.axis_index("seq")
    rows, channels = keys.shape
    half = rows // HALVES
    width = channels // CHUNKS
    modes = LANES * n
    right = lax.rem(me + 1, n)

    loads = [
        pltpu.make_async_copy(source, target, in_sem.at[i])
        for i, (source, target) in enumerate(
            (
                (filter_hbm, filt),
                (key_hbm, keys),
                (value_hbm, values),
                (first_hbm, first),
                (twist_hbm, twist),
                (middle_hbm, middle),
                (last_hbm, last),
            )
        )
    ]
    for load in loads:
        load.start()

    barrier = pltpu.get_barrier_semaphore()

    def greet(p, carry):
        pl.semaphore_signal(
            barrier, inc=1, device_id={"seq": lax.rem(me + p, n)}, device_id_type=MESH
        )
        return carry

    lax.fori_loop(1, n, greet, 0)

    def pack(slot, block):
        turned = jnp.transpose(block.astype(F32))
        parts = [
            turned[:, h * half : (h + 1) * half].reshape(n, 1, LANES, half)
            for h in range(HALVES)
        ]
        slabs = jnp.concatenate(parts, axis=1).reshape(n, HALVES * LANES, half)
        send[slot] = slabs.astype(BF16)

    def scatter(slot):
        def step(p, carry):
            peer = lax.rem(me + p, n)
            pltpu.make_async_remote_copy(
                src_ref=send.at[slot, peer],
                dst_ref=recv.at[slot, me],
                send_sem=send_sem.at[slot],
                recv_sem=recv_sem.at[slot],
                device_id={"seq": peer},
                device_id_type=MESH,
            ).start()
            return carry

        lax.fori_loop(1, n, step, 0)
        recv[slot, pl.ds(me, 1)] = send[slot, pl.ds(me, 1)]

    def arrived(slot):
        block = recv.at[slot, pl.ds(0, n - 1)]
        pltpu.make_async_copy(block, block, recv_sem.at[slot]).wait()

    def gone(slot):
        block = send.at[slot, pl.ds(0, n - 1)]
        pltpu.make_async_copy(block, block, send_sem.at[slot]).wait()

    def turn(part, h):
        table = twist[part, :, h * half : (h + 1) * half]
        return jnp.broadcast_to(table[None], (LANES, n, half)).reshape(modes, half)

    def forward(slot):
        block = recv[slot].reshape(n * HALVES * LANES, half)
        for h in range(HALVES):
            both = jnp.dot(first[h], block, preferred_element_type=F32)
            re, im = both[:modes], both[modes:]
            c, s = turn(0, h), turn(1, h)
            mixed[:, h * half : (h + 1) * half] = (re * c + im * s).astype(BF16)
            mixed[:, rows + h * half : rows + (h + 1) * half] = (im * c - re * s).astype(BF16)
        return (
            jnp.dot(mixed[...], middle[:, :rows], preferred_element_type=F32),
            jnp.dot(mixed[...], middle[:, rows:], preferred_element_type=F32),
        )

    loads[0].wait()
    pack(0, filt[:, :width])
    pl.semaphore_wait(barrier, n - 1)
    loads[1].wait()
    loads[2].wait()
    rims = [
        pltpu.make_async_remote_copy(
            src_ref=array.at[pl.ds(rows - 16, 16)],
            dst_ref=rim.at[i],
            send_sem=rim_send.at[i],
            recv_sem=rim_recv.at[i],
            device_id={"seq": right},
            device_id_type=MESH,
        )
        for i, array in enumerate((keys, values))
    ]
    for copy in rims:
        copy.start()
    scatter(0)
    pack(1, filt[:, width:])
    scatter(1)
    for copy in rims:
        copy.wait_recv()

    def short(samples, i, taps, columns):
        behind = rim[i, :, columns].astype(F32) * (me > 0).astype(F32)
        longer = jnp.concatenate([behind[8:], samples[:, columns].astype(F32)], axis=0)
        return (
            taps[0:1, columns] * longer[8:]
            + taps[1:2, columns] * longer[7 : rows + 7]
            + taps[2:3, columns] * longer[6 : rows + 6]
        )

    for q in range(CHUNKS):
        columns = slice(q * width, (q + 1) * width)
        gated = short(keys, 0, key_kernel, columns) * short(values, 1, value_kernel, columns)
        pack(2 + q, gated.astype(BF16))
        scatter(2 + q)

    for load in loads[3:]:
        load.wait()
    scale = 1.0 / (n * rows)
    for q in range(CHUNKS):
        arrived(q)
        re, im = forward(q)
        for c in range(LANES):
            gain = skip[q * width + me * LANES + c]
            spectrum[q, 0, c * n : (c + 1) * n] = (re[c * n : (c + 1) * n] + gain) * scale
        spectrum[q, 1] = im * scale

    for q in range(CHUNKS):
        arrived(2 + q)
        re, im = forward(2 + q)
        fre, fim = spectrum[q, 0], spectrum[q, 1]
        mixed[:, :rows] = (re * fim + im * fre).astype(BF16)
        mixed[:, rows:] = (re * fre - im * fim).astype(BF16)
        im = jnp.dot(mixed[...], middle[:, :rows], preferred_element_type=F32)
        re = jnp.dot(mixed[...], middle[:, rows:], preferred_element_type=F32)
        for h in range(HALVES):
            part = slice(h * half, (h + 1) * half)
            c, s = turn(0, h), turn(1, h)
            start = 2 * h * modes
            stacked[start : start + modes] = (re[:, part] * c - im[:, part] * s).astype(BF16)
            stacked[start + modes : start + 2 * modes] = (
                im[:, part] * c + re[:, part] * s
            ).astype(BF16)
        done = jnp.dot(last[...], stacked[...], preferred_element_type=F32)
        send[4 + q] = done.astype(BF16).reshape(n, HALVES * LANES, half)
        scatter(4 + q)

    stores = []
    for q in range(CHUNKS):
        arrived(4 + q)
        block = recv[4 + q].astype(F32).reshape(n, HALVES, LANES, half)
        columns = slice(q * width, (q + 1) * width)
        for h in range(HALVES):
            piece = block[:, h].reshape(width, half)
            out[h * half : (h + 1) * half, columns] = jnp.transpose(piece).astype(BF16)
        store = pltpu.make_async_copy(
            out.at[:, columns], out_hbm.at[:, columns], out_sem.at[q]
        )
        store.start()
        stores.append(store)

    for copy in rims:
        copy.wait_send()
    for slot in range(3 * CHUNKS):
        gone(slot)
    for store in stores:
        store.wait()


def on_device(n, key_rows, value_rows, key_kernel, value_kernel, long_filter, skip_gain):
    rows, channels = key_rows.shape
    half = rows // HALVES
    modes = LANES * n
    first, last, middle, twist = tables(n, rows)
    vmem = pl.BlockSpec(memory_space=pltpu.VMEM)
    smem = pl.BlockSpec(memory_space=pltpu.SMEM)
    hbm = pl.BlockSpec(memory_space=pl.ANY)
    slabs = (3 * CHUNKS, n, HALVES * LANES, half)
    return pl.pallas_call(
        functools.partial(kernel, n),
        out_shape=jax.ShapeDtypeStruct((rows, channels), BF16),
        in_specs=[hbm, hbm, vmem, vmem, hbm, smem, hbm, hbm, hbm, hbm],
        out_specs=hbm,
        scratch_shapes=[
            pltpu.VMEM((rows, channels), BF16),
            pltpu.VMEM((rows, channels), BF16),
            pltpu.VMEM((rows, channels), BF16),
            pltpu.VMEM(first.shape, BF16),
            pltpu.VMEM(last.shape, BF16),
            pltpu.VMEM(middle.shape, BF16),
            pltpu.VMEM(twist.shape, F32),
            pltpu.VMEM((2, 16, channels), BF16),
            pltpu.VMEM(slabs, BF16),
            pltpu.VMEM(slabs, BF16),
            pltpu.VMEM((CHUNKS, 2, modes, rows), F32),
            pltpu.VMEM((modes, 2 * rows), BF16),
            pltpu.VMEM((2 * HALVES * modes, half), BF16),
            pltpu.VMEM((rows, channels), BF16),
            pltpu.SemaphoreType.DMA((7,)),
            pltpu.SemaphoreType.DMA((2,)),
            pltpu.SemaphoreType.DMA((2,)),
            pltpu.SemaphoreType.DMA((3 * CHUNKS,)),
            pltpu.SemaphoreType.DMA((3 * CHUNKS,)),
            pltpu.SemaphoreType.DMA((CHUNKS,)),
        ],
        compiler_params=pltpu.CompilerParams(
            collective_id=0, has_side_effects=True, vmem_limit_bytes=40 * 1024 * 1024
        ),
    )(
        key_rows,
        value_rows,
        key_kernel,
        value_kernel,
        long_filter,
        skip_gain,
        jnp.asarray(first),
        jnp.asarray(last),
        jnp.asarray(middle),
        jnp.asarray(twist),
    )


def solution(mesh):
    return jax.shard_map(
        functools.partial(on_device, mesh.shape["seq"]),
        mesh=mesh,
        in_specs=(
            P("seq", "batch"),
            P("seq", "batch"),
            P(None, "batch"),
            P(None, "batch"),
            P("seq", "batch"),
            P("batch"),
        ),
        out_specs=P("seq", "batch"),
        check_vma=False,
    )
```

profile of v0, /device:TPU:1, one launch (start us, length us, event | category | flops | bytes accessed | tf_op | source)
XLA Modules:
  0.0 62.1 jit_solution(12516493862130932746)
XLA Ops:
  0.0 0.0 copy-start
  0.0 1.6 %copy-done = bf16[1024,1024]{1,0:T(8,128)(2,1)S(1)} copy-done((bf16[1024,1024]{1,0:T(8,128)(2,1)S(1)}, bf16[1024,1024]{1,0:T(8,128)(2,1)}, u32[]{:S(2)}) %copy-start) | copy-done | bytes 2097176
  1.6 0.0 copy-start.1
  1.6 1.2 %copy-done.1 = bf16[512,1024]{1,0:T(8,128)(2,1)S(1)} copy-done((bf16[512,1024]{1,0:T(8,128)(2,1)S(1)}, bf16[512,1024]{1,0:T(8,128)(2,1)}, u32[]{:S(2)}) %copy-start.1) | copy-done | bytes 1048600
  2.8 0.0 copy-start.2
  2.8 1.2 %copy-done.2 = bf16[2,512,512]{2,1,0:T(8,128)(2,1)S(1)} copy-done((bf16[2,512,512]{2,1,0:T(8,128)(2,1)S(1)}, bf16[2,512,512]{2,1,0:T(8,128)(2,1)}, u32[]{:S(2)}) %copy-start.2) | copy-done | bytes 1048600
  4.0 0.0 copy-start.3
  4.0 1.0 %copy-done.3 = bf16[512,512]{1,0:T(8,128)(2,1)S(1)} copy-done((bf16[512,512]{1,0:T(8,128)(2,1)S(1)}, bf16[512,512]{1,0:T(8,128)(2,1)}, u32[]{:S(2)}) %copy-start.3) | copy-done | bytes 524312
  5.1 0.0 copy-start.4
  5.1 1.0 %copy-done.4 = bf16[512,512]{1,0:T(8,128)(2,1)S(1)} copy-done((bf16[512,512]{1,0:T(8,128)(2,1)S(1)}, bf16[512,512]{1,0:T(8,128)(2,1)}, u32[]{:S(2)}) %copy-start.4) | copy-done | bytes 524312
  6.1 0.0 copy-start.5
  6.1 1.0 %copy-done.5 = bf16[512,512]{1,0:T(8,128)(2,1)S(1)} copy-done((bf16[512,512]{1,0:T(8,128)(2,1)S(1)}, bf16[512,512]{1,0:T(8,128)(2,1)}, u32[]{:S(2)}) %copy-start.5) | copy-done | bytes 524312
  7.2 0.0 copy-start.6
  7.2 0.9 %copy-done.6 = f32[2,32,512]{2,1,0:T(8,128)S(1)} copy-done((f32[2,32,512]{2,1,0:T(8,128)S(1)}, f32[2,32,512]{2,1,0:T(8,128)}, u32[]{:S(2)}) %copy-start.6) | copy-done | bytes 131096
  8.1 0.0 copy-start.7
  8.1 0.7 %copy-done.7 = f32[3,512]{1,0:T(4,128)S(1)} copy-done((f32[3,512]{1,0:T(4,128)S(1)}, f32[3,512]{1,0:T(4,128)}, u32[]{:S(2)}) %copy-start.7) | copy-done | bytes 6168
  8.8 0.0 copy-start.8
  8.8 0.7 %copy-done.8 = f32[3,512]{1,0:T(4,128)S(1)} copy-done((f32[3,512]{1,0:T(4,128)S(1)}, f32[3,512]{1,0:T(4,128)}, u32[]{:S(2)}) %copy-start.8) | copy-done | bytes 6168
  9.5 0.0 copy-start.9
  9.5 0.7 %copy-done.9 = f32[512]{0:T(512)S(1)} copy-done((f32[512]{0:T(512)S(1)}, f32[512]{0:T(512)}, u32[]{:S(2)}) %copy-start.9) | copy-done | bytes 2072
  10.2 51.2 %shard_map.100 = bf16[512,512]{1,0:T(8,128)(2,1)S(1)} custom-call(bf16[512,512]{1,0:T(8,128)(2,1)S(1)} %copy-done.3, bf16[512,512]{1,0:T(8,128)(2,1)S(1)} %copy-done.4, f32[3,512]{1,0:T(4,128)S(1)} %copy-done.7, f32[3,512]{1,0:T(4,128)S(1)} %copy-done.8, bf16[512,512]{1,0:T(8,128)(2,1)S(1)} %copy-done.5, f32[512]{0:T(512)S(1)} %copy-done.9, ...), custom_call_target="tpu_custom_call" | custom-call | tf_op jit(solution)/shard_map/pallas_call | solution.py:262
  61.3 0.8 %copy.12 = bf16[512,512]{1,0:T(8,128)(2,1)} copy(bf16[512,512]{1,0:T(8,128)(2,1)S(1)} %shard_map.100) | data formatting | bytes 1048576
Async XLA Ops:
  0.0 1.6 %copy-start = (bf16[1024,1024]{1,0:T(8,128)(2,1)S(1)}, bf16[1024,1024]{1,0:T(8,128)(2,1)}, u32[]{:S(2)}) copy-start(bf16[1024,1024]{1,0:T(8,128)(2,1)} %constant.10.clone.middle_hbm) | copy-start | bytes 6291460
  1.6 1.2 %copy-start.1 = (bf16[512,1024]{1,0:T(8,128)(2,1)S(1)}, bf16[512,1024]{1,0:T(8,128)(2,1)}, u32[]{:S(2)}) copy-start(bf16[512,1024]{1,0:T(8,128)(2,1)} %constant.9.clone.last_hbm) | copy-start | bytes 3145732
  2.8 1.2 %copy-start.2 = (bf16[2,512,512]{2,1,0:T(8,128)(2,1)S(1)}, bf16[2,512,512]{2,1,0:T(8,128)(2,1)}, u32[]{:S(2)}) copy-start(bf16[2,512,512]{2,1,0:T(8,128)(2,1)} %constant.8.clone.first_hbm) | copy-start | bytes 3145732
  4.0 1.0 %copy-start.3 = (bf16[512,512]{1,0:T(8,128)(2,1)S(1)}, bf16[512,512]{1,0:T(8,128)(2,1)}, u32[]{:S(2)}) copy-start(bf16[512,512]{1,0:T(8,128)(2,1)} %key_hbm.1) | copy-start | bytes 1572868
  5.1 1.0 %copy-start.4 = (bf16[512,512]{1,0:T(8,128)(2,1)S(1)}, bf16[512,512]{1,0:T(8,128)(2,1)}, u32[]{:S(2)}) copy-start(bf16[512,512]{1,0:T(8,128)(2,1)} %value_hbm.1) | copy-start | bytes 1572868
  6.1 1.0 %copy-start.5 = (bf16[512,512]{1,0:T(8,128)(2,1)S(1)}, bf16[512,512]{1,0:T(8,128)(2,1)}, u32[]{:S(2)}) copy-start(bf16[512,512]{1,0:T(8,128)(2,1)} %filter_hbm.1) | copy-start | bytes 1572868
  7.2 0.9 %copy-start.6 = (f32[2,32,512]{2,1,0:T(8,128)S(1)}, f32[2,32,512]{2,1,0:T(8,128)}, u32[]{:S(2)}) copy-start(f32[2,32,512]{2,1,0:T(8,128)} %constant.11.clone.twist_hbm) | copy-start | bytes 393220
  8.1 0.7 %copy-start.7 = (f32[3,512]{1,0:T(4,128)S(1)}, f32[3,512]{1,0:T(4,128)}, u32[]{:S(2)}) copy-start(f32[3,512]{1,0:T(4,128)} %key_kernel.1) | copy-start | bytes 18436
  8.8 0.7 %copy-start.8 = (f32[3,512]{1,0:T(4,128)S(1)}, f32[3,512]{1,0:T(4,128)}, u32[]{:S(2)}) copy-start(f32[3,512]{1,0:T(4,128)} %value_kernel.1) | copy-start | bytes 18436
  9.5 0.7 %copy-start.9 = (f32[512]{0:T(512)S(1)}, f32[512]{0:T(512)}, u32[]{:S(2)}) copy-start(f32[512]{0:T(512)} %skip.1) | copy-start | bytes 6148
where the time goes:
time: 62.6 us; the launch traced here: 62.1 us
  Pallas kernels  51.2 us (82%)
  local copies, waits for them, and re-layouts  10.9 us (17%)
    pallas_call x1, Pallas kernels, on_device(): pl.pallas_call(functools.partial(kernel, n), out_shape=jax.ShapeDtypeStru...  51.2 us
    unnamed x21, local copies, waits for them, and re-layouts  10.9 us

commit v1 on v0

--- a/solution.py
+++ b/solution.py
@@ -52,7 +52,7 @@
     last_hbm,
     middle_hbm,
     twist_hbm,
-    out_hbm,
+    out,
     keys,
     values,
     filt,
@@ -66,13 +66,11 @@
     spectrum,
     mixed,
     stacked,
-    out,
     in_sem,
     rim_send,
     rim_recv,
     send_sem,
     recv_sem,
-    out_sem,
 ):
     me = lax.axis_index("seq")
     rows, channels = keys.shape
@@ -80,6 +78,16 @@
     width = channels // CHUNKS
     modes = LANES * n
     right = lax.rem(me + 1, n)
+
+    barrier = pltpu.get_barrier_semaphore()
+
+    def greet(p, carry):
+        pl.semaphore_signal(
+            barrier, inc=1, device_id={"seq": lax.rem(me + p, n)}, device_id_type=MESH
+        )
+        return carry
+
+    lax.fori_loop(1, n, greet, 0)
 
     loads = [
         pltpu.make_async_copy(source, target, in_sem.at[i])
@@ -97,16 +105,6 @@
     ]
     for load in loads:
         load.start()
-
-    barrier = pltpu.get_barrier_semaphore()
-
-    def greet(p, carry):
-        pl.semaphore_signal(
-            barrier, inc=1, device_id={"seq": lax.rem(me + p, n)}, device_id_type=MESH
-        )
-        return carry
-
-    lax.fori_loop(1, n, greet, 0)
 
     def pack(slot, block):
         turned = jnp.transpose(block.astype(F32))
@@ -178,7 +176,6 @@
         copy.start()
     scatter(0)
     pack(1, filt[:, width:])
-    scatter(1)
     for copy in rims:
         copy.wait_recv()
 
@@ -196,6 +193,8 @@
         gated = short(keys, 0, key_kernel, columns) * short(values, 1, value_kernel, columns)
         pack(2 + q, gated.astype(BF16))
         scatter(2 + q)
+        if q == 0:
+            scatter(1)
 
     for load in loads[3:]:
         load.wait()
@@ -228,7 +227,6 @@
         send[4 + q] = done.astype(BF16).reshape(n, HALVES * LANES, half)
         scatter(4 + q)
 
-    stores = []
     for q in range(CHUNKS):
         arrived(4 + q)
         block = recv[4 + q].astype(F32).reshape(n, HALVES, LANES, half)
@@ -236,18 +234,11 @@
         for h in range(HALVES):
             piece = block[:, h].reshape(width, half)
             out[h * half : (h + 1) * half, columns] = jnp.transpose(piece).astype(BF16)
-        store = pltpu.make_async_copy(
-            out.at[:, columns], out_hbm.at[:, columns], out_sem.at[q]
-        )
-        store.start()
-        stores.append(store)
 
     for copy in rims:
         copy.wait_send()
     for slot in range(3 * CHUNKS):
         gone(slot)
-    for store in stores:
-        store.wait()
 
 
 def on_device(n, key_rows, value_rows, key_kernel, value_kernel, long_filter, skip_gain):
@@ -257,13 +248,13 @@
     first, last, middle, twist = tables(n, rows)
     vmem = pl.BlockSpec(memory_space=pltpu.VMEM)
     smem = pl.BlockSpec(memory_space=pltpu.SMEM)
-    hbm = pl.BlockSpec(memory_space=pl.ANY)
+    hbm = pl.BlockSpec(memory_space=pltpu.HBM)
     slabs = (3 * CHUNKS, n, HALVES * LANES, half)
     return pl.pallas_call(
         functools.partial(kernel, n),
-        out_shape=jax.ShapeDtypeStruct((rows, channels), BF16),
+        out_shape=pltpu.VMEM((rows, channels), BF16),
         in_specs=[hbm, hbm, vmem, vmem, hbm, smem, hbm, hbm, hbm, hbm],
-        out_specs=hbm,
+        out_specs=vmem,
         scratch_shapes=[
             pltpu.VMEM((rows, channels), BF16),
             pltpu.VMEM((rows, channels), BF16),
@@ -278,16 +269,14 @@
             pltpu.VMEM((CHUNKS, 2, modes, rows), F32),
             pltpu.VMEM((modes, 2 * rows), BF16),
             pltpu.VMEM((2 * HALVES * modes, half), BF16),
-            pltpu.VMEM((rows, channels), BF16),
             pltpu.SemaphoreType.DMA((7,)),
             pltpu.SemaphoreType.DMA((2,)),
             pltpu.SemaphoreType.DMA((2,)),
             pltpu.SemaphoreType.DMA((3 * CHUNKS,)),
             pltpu.SemaphoreType.DMA((3 * CHUNKS,)),
-            pltpu.SemaphoreType.DMA((CHUNKS,)),
         ],
         compiler_params=pltpu.CompilerParams(
-            collective_id=0, has_side_effects=True, vmem_limit_bytes=40 * 1024 * 1024
+            collective_id=0, has_side_effects=True, vmem_limit_bytes=63 * 1024 * 1024
         ),
     )(
         key_rows,

time: 62.6 us -> 52.2 us (0.83)
  local copies, waits for them, and re-layouts: 10.9 us -> 0.8 us
    unnamed x21 -> x1, local copies, waits for them, and re-layouts: 10.9 us -> 0.8 us
where the time goes in v1:
time: 52.2 us; the launch traced here: 52 us
  Pallas kernels  51.2 us (98%)
  local copies, waits for them, and re-layouts  0.8 us (2%)
    pallas_call x1, Pallas kernels, on_device(): pl.pallas_call(functools.partial(kernel, n), out_shape=pltpu.VMEM((rows,...  51.2 us

profile of v1, /device:TPU:1, one launch (start us, length us, event | category | flops | bytes accessed | tf_op | source)
XLA Modules:
  0.0 52.0 jit_solution(3737723039588675936)
XLA Ops:
  0.0 51.2 %shard_map.100 = bf16[512,512]{1,0:T(8,128)(2,1)S(1)} custom-call(bf16[512,512]{1,0:T(8,128)(2,1)} %key_hbm.1, bf16[512,512]{1,0:T(8,128)(2,1)} %value_hbm.1, f32[3,512]{1,0:T(4,128)} %key_kernel.1, f32[3,512]{1,0:T(4,128)} %value_kernel.1, bf16[512,512]{1,0:T(8,128)(2,1)} %filter_hbm.1, f32[512]{0:T(512)} %skip.1, ...), custom_call_target="tpu_custom_call" | custom-call | tf_op jit(solution)/shard_map/pallas_call | solution.py:253
  51.2 0.8 %copy.12 = bf16[512,512]{1,0:T(8,128)(2,1)} copy(bf16[512,512]{1,0:T(8,128)(2,1)S(1)} %shard_map.100) | data formatting | bytes 1048576

commit v2 on v1

v2 whole, which is shorter than its diff:
```python
import functools
import math

import jax
import jax.numpy as jnp
import numpy as np
from jax import lax
from jax.experimental import pallas as pl
from jax.experimental.pallas import tpu as pltpu
from jax.sharding import PartitionSpec as P

import ml_dtypes

MESH = pl.DeviceIdType.MESH
F32 = jnp.float32
BF16 = jnp.bfloat16
CHUNKS = 4
LANES = 4
PIECES = 4


def tables(n, rows):
    length = n * rows
    piece_rows = rows // PIECES
    outer = 2.0 * math.pi * np.outer(np.arange(n) + 0.25, np.arange(n)) / n
    pair = np.stack([np.cos(outer), -np.sin(outer)])
    first = np.einsum("pks,hg,cd->hpcksgd", pair, np.eye(PIECES), np.eye(LANES))
    first = first.reshape(PIECES * 2 * LANES * n, n * PIECES * LANES)
    last = first.T
    inner = 2.0 * math.pi * (np.outer(np.arange(rows), np.arange(rows)) % rows) / rows
    c, s = np.cos(inner), np.sin(inner)
    middle = np.block([[c, -s], [s, c]])
    order = np.einsum("de,hg,cb->dhcgeb", np.eye(n), np.eye(PIECES), np.eye(LANES))
    order = order.reshape(n * PIECES * LANES, -1)
    twist = 2.0 * math.pi * np.outer(np.arange(n) + 0.25, np.arange(rows)) / length
    low = lambda a: np.ascontiguousarray(a).astype(ml_dtypes.bfloat16)
    return (
        low(first),
        low(last),
        low(middle),
        low(order),
        np.stack([np.cos(twist), np.sin(twist)]).astype(np.float32),
    )


def kernel(
    n,
    key_hbm,
    value_hbm,
    key_kernel,
    value_kernel,
    filter_hbm,
    skip,
    first_hbm,
    last_hbm,
    middle_hbm,
    order_hbm,
    twist_hbm,
    out,
    keys,
    values,
    filt,
    first,
    last,
    middle,
    order,
    twist,
    rim,
    send,
    recv,
    spectrum,
    mixed,
    stacked,
    in_sem,
    rim_send,
    rim_recv,
    send_sem,
    recv_sem,
):
    me = lax.axis_index("seq")
    planes = n // 4
    my_side, my_plane, my_core = me // (2 * planes), (me // 2) % planes, me % 2
    rows, channels = keys.shape
    piece_rows = rows // PIECES
    width = channels // CHUNKS
    modes = LANES * n
    right = lax.rem(me + 1, n)

    barrier = pltpu.get_barrier_semaphore()

    def greet(p, carry):
        pl.semaphore_signal(
            barrier, inc=1, device_id={"seq": lax.rem(me + p, n)}, device_id_type=MESH
        )
        return carry

    lax.fori_loop(1, n, greet, 0)

    loads = [
        pltpu.make_async_copy(source, target, in_sem.at[i])
        for i, (source, target) in enumerate(
            (
                (filter_hbm, filt),
                (order_hbm, order),
                (key_hbm, keys),
                (value_hbm, values),
                (first_hbm, first),
                (twist_hbm, twist),
                (middle_hbm, middle),
                (last_hbm, last),
            )
        )
    ]
    for load in loads:
        load.start()

    def pack(slot, block):
        parts = [block[h * piece_rows : (h + 1) * piece_rows] for h in range(PIECES)]
        slabs = lax.dot_general(
            order[...],
            jnp.concatenate(parts, axis=1),
            (((1,), (1,)), ((), ())),
            preferred_element_type=F32,
        )
        send[slot] = slabs.astype(BF16).reshape(n, PIECES * LANES, piece_rows)

    def flip(place, other):
        return 1 - place if other else place

    def send_to(slot, peer):
        pltpu.make_async_remote_copy(
            src_ref=send.at[slot, peer],
            dst_ref=recv.at[slot, me],
            send_sem=send_sem.at[slot],
            recv_sem=recv_sem.at[slot],
            device_id={"seq": peer},
            device_id_type=MESH,
        ).start()

    def scatter(slot):
        def step(i, carry):
            shift = (i + 1) // 2
            distance = planes // 2 + jnp.where(i % 2 == 1, -shift, shift)
            plane = my_plane + distance
            plane = jnp.where(plane >= planes, plane - planes, plane)
            for side in (1, 0):
                for core in (1, 0):
                    send_to(slot, flip(my_side, side) * 2 * planes + plane * 2 + flip(my_core, core))
            return carry

        lax.fori_loop(0, planes - 1, step, 0)
        for side, core in ((1, 1), (1, 0), (0, 1)):
            send_to(slot, flip(my_side, side) * 2 * planes + my_plane * 2 + flip(my_core, core))
        recv[slot, pl.ds(me, 1)] = send[slot, pl.ds(me, 1)]

    def arrived(slot):
        block = recv.at[slot, pl.ds(0, n - 1)]
        pltpu.make_async_copy(block, block, recv_sem.at[slot]).wait()

    def gone(slot):
        block = send.at[slot, pl.ds(0, n - 1)]
        pltpu.make_async_copy(block, block, send_sem.at[slot]).wait()

    def turn(part, h):
        table = twist[part, :, h * piece_rows : (h + 1) * piece_rows]
        return jnp.broadcast_to(table[None], (LANES, n, piece_rows)).reshape(modes, piece_rows)

    def forward(slot):
        block = recv[slot].reshape(n * PIECES * LANES, piece_rows)
        both = jnp.dot(first[...], block, preferred_element_type=F32)
        for h in range(PIECES):
            start = 2 * h * modes
            re, im = both[start : start + modes], both[start + modes : start + 2 * modes]
            c, s = turn(0, h), turn(1, h)
            mixed[:, h * piece_rows : (h + 1) * piece_rows] = (re * c + im * s).astype(BF16)
            mixed[:, rows + h * piece_rows : rows + (h + 1) * piece_rows] = (
                im * c - re * s
            ).astype(BF16)
        both = jnp.dot(mixed[...], middle[...], preferred_element_type=F32)
        return both[:, :rows], both[:, rows:]

    loads[0].wait()
    loads[1].wait()
    pack(0, filt[:, :width])
    pl.semaphore_wait(barrier, n - 1)
    loads[2].wait()
    loads[3].wait()
    rims = [
        pltpu.make_async_remote_copy(
            src_ref=array.at[pl.ds(rows - 16, 16)],
            dst_ref=rim.at[i],
            send_sem=rim_send.at[i],
            recv_sem=rim_recv.at[i],
            device_id={"seq": right},
            device_id_type=MESH,
        )
        for i, array in enumerate((keys, values))
    ]
    for copy in rims:
        copy.start()
    scatter(0)
    for copy in rims:
        copy.wait_recv()

    def short(samples, i, taps, columns):
        behind = rim[i, :, columns].astype(F32) * (me > 0).astype(F32)
        longer = jnp.concatenate([behind[8:], samples[:, columns].astype(F32)], axis=0)
        return (
            taps[0:1, columns] * longer[8:]
            + taps[1:2, columns] * longer[7 : rows + 7]
            + taps[2:3, columns] * longer[6 : rows + 6]
        )

    for q in range(CHUNKS):
        columns = slice(q * width, (q + 1) * width)
        if q:
            pack(q, filt[:, columns])
            scatter(q)
        gated = short(keys, 0, key_kernel, columns) * short(values, 1, value_kernel, columns)
        pack(CHUNKS + q, gated.astype(BF16))
        scatter(CHUNKS + q)

    for load in loads[4:]:
        load.wait()
    scale = 1.0 / (n * rows)
    for q in range(CHUNKS):
        arrived(q)
        re, im = forward(q)
        for c in range(LANES):
            gain = skip[q * width + me * LANES + c]
            spectrum[0, c * n : (c + 1) * n] = (re[c * n : (c + 1) * n] + gain) * scale
        spectrum[1] = im * scale

        arrived(CHUNKS + q)
        re, im = forward(CHUNKS + q)
        fre, fim = spectrum[0], spectrum[1]
        mixed[:, :rows] = (re * fim + im * fre).astype(BF16)
        mixed[:, rows:] = (re * fre - im * fim).astype(BF16)
        both = jnp.dot(mixed[...], middle[...], preferred_element_type=F32)
        im, re = both[:, :rows], both[:, rows:]
        for h in range(PIECES):
            part = slice(h * piece_rows, (h + 1) * piece_rows)
            c, s = turn(0, h), turn(1, h)
            start = 2 * h * modes
            stacked[start : start + modes] = (re[:, part] * c - im[:, part] * s).astype(BF16)
            stacked[start + modes : start + 2 * modes] = (
                im[:, part] * c + re[:, part] * s
            ).astype(BF16)
        done = jnp.dot(last[...], stacked[...], preferred_element_type=F32)
        send[2 * CHUNKS + q] = done.astype(BF16).reshape(n, PIECES * LANES, piece_rows)
        scatter(2 * CHUNKS + q)

    for q in range(CHUNKS):
        arrived(2 * CHUNKS + q)
        block = recv[2 * CHUNKS + q].reshape(n * PIECES * LANES, piece_rows)
        turned = lax.dot_general(
            block, order[...], (((0,), (0,)), ((), ())), preferred_element_type=F32
        )
        for h in range(PIECES):
            out[h * piece_rows : (h + 1) * piece_rows, q * width : (q + 1) * width] = turned[
                :, h * width : (h + 1) * width
            ].astype(BF16)

    for copy in rims:
        copy.wait_send()
    for slot in range(3 * CHUNKS):
        gone(slot)


def on_device(n, key_rows, value_rows, key_kernel, value_kernel, long_filter, skip_gain):
    rows, channels = key_rows.shape
    piece_rows = rows // PIECES
    modes = LANES * n
    first, last, middle, order, twist = tables(n, rows)
    vmem = pl.BlockSpec(memory_space=pltpu.VMEM)
    smem = pl.BlockSpec(memory_space=pltpu.SMEM)
    hbm = pl.BlockSpec(memory_space=pltpu.HBM)
    slabs = (3 * CHUNKS, n, PIECES * LANES, piece_rows)
    return pl.pallas_call(
        functools.partial(kernel, n),
        out_shape=pltpu.VMEM((rows, channels), BF16),
        in_specs=[hbm, hbm, vmem, vmem, hbm, smem, hbm, hbm, hbm, hbm, hbm],
        out_specs=vmem,
        scratch_shapes=[
            pltpu.VMEM((rows, channels), BF16),
            pltpu.VMEM((rows, channels), BF16),
            pltpu.VMEM((rows, channels), BF16),
            pltpu.VMEM(first.shape, BF16),
            pltpu.VMEM(last.shape, BF16),
            pltpu.VMEM(middle.shape, BF16),
            pltpu.VMEM(order.shape, BF16),
            pltpu.VMEM(twist.shape, F32),
            pltpu.VMEM((2, 16, channels), BF16),
            pltpu.VMEM(slabs, BF16),
            pltpu.VMEM(slabs, BF16),
            pltpu.VMEM((2, modes, rows), F32),
            pltpu.VMEM((modes, 2 * rows), BF16),
            pltpu.VMEM((2 * PIECES * modes, piece_rows), BF16),
            pltpu.SemaphoreType.DMA((8,)),
            pltpu.SemaphoreType.DMA((2,)),
            pltpu.SemaphoreType.DMA((2,)),
            pltpu.SemaphoreType.DMA((3 * CHUNKS,)),
            pltpu.SemaphoreType.DMA((3 * CHUNKS,)),
        ],
        compiler_params=pltpu.CompilerParams(
            collective_id=0, has_side_effects=True, vmem_limit_bytes=63 * 1024 * 1024
        ),
    )(
        key_rows,
        value_rows,
        key_kernel,
        value_kernel,
        long_filter,
        skip_gain,
        jnp.asarray(first),
        jnp.asarray(last),
        jnp.asarray(middle),
        jnp.asarray(order),
        jnp.asarray(twist),
    )


def solution(mesh):
    return jax.shard_map(
        functools.partial(on_device, mesh.shape["seq"]),
        mesh=mesh,
        in_specs=(
            P("seq", "batch"),
            P("seq", "batch"),
            P(None, "batch"),
            P(None, "batch"),
            P("seq", "batch"),
            P("batch"),
        ),
        out_specs=P("seq", "batch"),
        check_vma=False,
    )
```

time: 52.2 us -> 49.2 us (0.943)
  Pallas kernels: 51.2 us -> 48.3 us
    pallas_call x1, Pallas kernels: 51.2 us -> 48.3 us  [on_device(): pl.pallas_call(functools.partial(kernel, n), out_shape=pltpu.VMEM((rows,...]
where the time goes in v2:
time: 49.2 us; the launch traced here: 49.1 us
  Pallas kernels  48.3 us (98%)
  local copies, waits for them, and re-layouts  0.8 us (2%)
    pallas_call x1, Pallas kernels, on_device(): pl.pallas_call(functools.partial(kernel, n), out_shape=pltpu.VMEM((rows,...  48.3 us

profile of v2, /device:TPU:1, one launch (start us, length us, event | category | flops | bytes accessed | tf_op | source)
XLA Modules:
  0.0 49.1 jit_solution(14252643796537774261)
XLA Ops:
  0.0 48.3 %shard_map.109 = bf16[512,512]{1,0:T(8,128)(2,1)S(1)} custom-call(bf16[512,512]{1,0:T(8,128)(2,1)} %key_hbm.1, bf16[512,512]{1,0:T(8,128)(2,1)} %value_hbm.1, f32[3,512]{1,0:T(4,128)} %key_kernel.1, f32[3,512]{1,0:T(4,128)} %value_kernel.1, bf16[512,512]{1,0:T(8,128)(2,1)} %filter_hbm.1, f32[512]{0:T(512)} %skip.1, ...), custom_call_target="tpu_custom_call" | custom-call | tf_op jit(solution)/shard_map/pallas_call | solution.py:279
  48.3 0.8 %copy.13 = bf16[512,512]{1,0:T(8,128)(2,1)} copy(bf16[512,512]{1,0:T(8,128)(2,1)S(1)} %shard_map.109) | data formatting | bytes 1048576

commit v3 on v2

--- a/solution.py
+++ b/solution.py
@@ -47,10 +47,10 @@
     n,
     key_hbm,
     value_hbm,
-    key_kernel,
-    value_kernel,
+    key_taps_hbm,
+    value_taps_hbm,
     filter_hbm,
-    skip,
+    skip_hbm,
     first_hbm,
     last_hbm,
     middle_hbm,
@@ -60,6 +60,9 @@
     keys,
     values,
     filt,
+    key_taps,
+    value_taps,
+    skip,
     first,
     last,
     middle,
@@ -88,13 +91,29 @@
 
     barrier = pltpu.get_barrier_semaphore()
 
-    def greet(p, carry):
-        pl.semaphore_signal(
-            barrier, inc=1, device_id={"seq": lax.rem(me + p, n)}, device_id_type=MESH
-        )
-        return carry
-
-    lax.fori_loop(1, n, greet, 0)
+    def flip(place, other):
+        return 1 - place if other else place
+
+    def each_peer(act):
+        def step(i, carry):
+            shift = (i + 1) // 2
+            distance = planes // 2 + jnp.where(i % 2 == 1, -shift, shift)
+            plane = my_plane + distance
+            plane = jnp.where(plane >= planes, plane - planes, plane)
+            for side in (1, 0):
+                for core in (1, 0):
+                    act(flip(my_side, side) * 2 * planes + plane * 2 + flip(my_core, core))
+            return carry
+
+        lax.fori_loop(0, planes - 1, step, 0)
+        for side, core in ((1, 1), (1, 0), (0, 1)):
+            act(flip(my_side, side) * 2 * planes + my_plane * 2 + flip(my_core, core))
+
+    each_peer(
+        lambda peer: pl.semaphore_signal(
+            barrier, inc=1, device_id={"seq": peer}, device_id_type=MESH
+        )
+    )
 
     loads = [
         pltpu.make_async_copy(source, target, in_sem.at[i])
@@ -104,6 +123,9 @@
                 (order_hbm, order),
                 (key_hbm, keys),
                 (value_hbm, values),
+                (key_taps_hbm, key_taps),
+                (value_taps_hbm, value_taps),
+                (skip_hbm, skip),
                 (first_hbm, first),
                 (twist_hbm, twist),
                 (middle_hbm, middle),
@@ -123,9 +145,6 @@
             preferred_element_type=F32,
         )
         send[slot] = slabs.astype(BF16).reshape(n, PIECES * LANES, piece_rows)
-
-    def flip(place, other):
-        return 1 - place if other else place
 
     def send_to(slot, peer):
         pltpu.make_async_remote_copy(
@@ -138,19 +157,7 @@
         ).start()
 
     def scatter(slot):
-        def step(i, carry):
-            shift = (i + 1) // 2
-            distance = planes // 2 + jnp.where(i % 2 == 1, -shift, shift)
-            plane = my_plane + distance
-            plane = jnp.where(plane >= planes, plane - planes, plane)
-            for side in (1, 0):
-                for core in (1, 0):
-                    send_to(slot, flip(my_side, side) * 2 * planes + plane * 2 + flip(my_core, core))
-            return carry
-
-        lax.fori_loop(0, planes - 1, step, 0)
-        for side, core in ((1, 1), (1, 0), (0, 1)):
-            send_to(slot, flip(my_side, side) * 2 * planes + my_plane * 2 + flip(my_core, core))
+        each_peer(functools.partial(send_to, slot))
         recv[slot, pl.ds(me, 1)] = send[slot, pl.ds(me, 1)]
 
     def arrived(slot):
@@ -199,6 +206,8 @@
     for copy in rims:
         copy.start()
     scatter(0)
+    for load in loads[4:6]:
+        load.wait()
     for copy in rims:
         copy.wait_recv()
 
@@ -216,11 +225,11 @@
         if q:
             pack(q, filt[:, columns])
             scatter(q)
-        gated = short(keys, 0, key_kernel, columns) * short(values, 1, value_kernel, columns)
+        gated = short(keys, 0, key_taps, columns) * short(values, 1, value_taps, columns)
         pack(CHUNKS + q, gated.astype(BF16))
         scatter(CHUNKS + q)
 
-    for load in loads[4:]:
+    for load in loads[6:]:
         load.wait()
     scale = 1.0 / (n * rows)
     for q in range(CHUNKS):
@@ -273,18 +282,20 @@
     modes = LANES * n
     first, last, middle, order, twist = tables(n, rows)
     vmem = pl.BlockSpec(memory_space=pltpu.VMEM)
-    smem = pl.BlockSpec(memory_space=pltpu.SMEM)
     hbm = pl.BlockSpec(memory_space=pltpu.HBM)
     slabs = (3 * CHUNKS, n, PIECES * LANES, piece_rows)
     return pl.pallas_call(
         functools.partial(kernel, n),
         out_shape=pltpu.VMEM((rows, channels), BF16),
-        in_specs=[hbm, hbm, vmem, vmem, hbm, smem, hbm, hbm, hbm, hbm, hbm],
+        in_specs=[hbm] * 11,
         out_specs=vmem,
         scratch_shapes=[
             pltpu.VMEM((rows, channels), BF16),
             pltpu.VMEM((rows, channels), BF16),
             pltpu.VMEM((rows, channels), BF16),
+            pltpu.VMEM(key_kernel.shape, F32),
+            pltpu.VMEM(value_kernel.shape, F32),
+            pltpu.SMEM(skip_gain.shape, F32),
             pltpu.VMEM(first.shape, BF16),
             pltpu.VMEM(last.shape, BF16),
             pltpu.VMEM(middle.shape, BF16),
@@ -296,7 +307,7 @@
             pltpu.VMEM((2, modes, rows), F32),
             pltpu.VMEM((modes, 2 * rows), BF16),
             pltpu.VMEM((2 * PIECES * modes, piece_rows), BF16),
-            pltpu.SemaphoreType.DMA((8,)),
+            pltpu.SemaphoreType.DMA((11,)),
             pltpu.SemaphoreType.DMA((2,)),
             pltpu.SemaphoreType.DMA((2,)),
             pltpu.SemaphoreType.DMA((3 * CHUNKS,)),

time: 49.2 us -> 47.9 us (0.974)
  Pallas kernels: 48.3 us -> 47 us
    pallas_call x1, Pallas kernels: 48.3 us -> 47 us  [on_device(): pl.pallas_call(functools.partial(kernel, n), out_shape=pltpu.VMEM((rows,...]
where the time goes in v3:
time: 47.9 us
  Pallas kernels  47 us (98%)
  local copies, waits for them, and re-layouts  0.8 us (2%)
    pallas_call x1, Pallas kernels, on_device(): pl.pallas_call(functools.partial(kernel, n), out_shape=pltpu.VMEM((rows,...  47 us

profile of v3, /device:TPU:1, one launch (start us, length us, event | category | flops | bytes accessed | tf_op | source)
XLA Modules:
  0.0 47.9 jit_solution(11957872247649253601)
XLA Ops:
  0.0 47.0 %shard_map.109 = bf16[512,512]{1,0:T(8,128)(2,1)S(1)} custom-call(bf16[512,512]{1,0:T(8,128)(2,1)} %key_hbm.1, bf16[512,512]{1,0:T(8,128)(2,1)} %value_hbm.1, f32[3,512]{1,0:T(4,128)} %key_taps_hbm.1, f32[3,512]{1,0:T(4,128)} %value_taps_hbm.1, bf16[512,512]{1,0:T(8,128)(2,1)} %filter_hbm.1, f32[512]{0:T(512)} %skip_hbm.1, ...), custom_call_target="tpu_custom_call" | custom-call | tf_op jit(solution)/shard_map/pallas_call | solution.py:287
  47.1 0.8 %copy.13 = bf16[512,512]{1,0:T(8,128)(2,1)} copy(bf16[512,512]{1,0:T(8,128)(2,1)S(1)} %shard_map.109) | data formatting | bytes 1048576

commit v4 on v3

--- a/solution.py
+++ b/solution.py
@@ -79,6 +79,7 @@
     rim_recv,
     send_sem,
     recv_sem,
+    told,
 ):
     me = lax.axis_index("seq")
     planes = n // 4
@@ -106,14 +107,31 @@
             return carry
 
         lax.fori_loop(0, planes - 1, step, 0)
+        same_plane(act)
+
+    def at_distances(distances, act):
+        for distance in distances:
+            plane = my_plane + distance % planes
+            plane = jnp.where(plane >= planes, plane - planes, plane)
+            for side in (1, 0):
+                for core in (1, 0):
+                    act(flip(my_side, side) * 2 * planes + plane * 2 + flip(my_core, core))
+
+    def same_plane(act):
         for side, core in ((1, 1), (1, 0), (0, 1)):
             act(flip(my_side, side) * 2 * planes + my_plane * 2 + flip(my_core, core))
 
-    each_peer(
-        lambda peer: pl.semaphore_signal(
-            barrier, inc=1, device_id={"seq": peer}, device_id_type=MESH
-        )
-    )
+    def column(distance):
+        plane = my_plane + distance % planes
+        plane = jnp.where(plane >= planes, plane - planes, plane)
+        return my_side * 2 * planes + plane * 2 + my_core
+
+    def signal(semaphore, peer):
+        pl.semaphore_signal(semaphore, inc=1, device_id={"seq": peer}, device_id_type=MESH)
+
+    near, far = (2, -2, 1, -1), (3, -3)
+    at_distances(near, functools.partial(signal, barrier))
+    same_plane(functools.partial(signal, barrier))
 
     loads = [
         pltpu.make_async_copy(source, target, in_sem.at[i])
@@ -156,9 +174,12 @@
             device_id_type=MESH,
         ).start()
 
+    def keep(slot):
+        recv[slot, pl.ds(me, 1)] = send[slot, pl.ds(me, 1)]
+
     def scatter(slot):
+        keep(slot)
         each_peer(functools.partial(send_to, slot))
-        recv[slot, pl.ds(me, 1)] = send[slot, pl.ds(me, 1)]
 
     def arrived(slot):
         block = recv.at[slot, pl.ds(0, n - 1)]
@@ -189,7 +210,10 @@
     loads[0].wait()
     loads[1].wait()
     pack(0, filt[:, :width])
-    pl.semaphore_wait(barrier, n - 1)
+    pl.semaphore_wait(barrier, 4 * (len(near) + 1) - 1)
+    signal(told.at[0], column(-1))
+    signal(told.at[1], column(1))
+    signal(told.at[2], column(-2))
     loads[2].wait()
     loads[3].wait()
     rims = [
@@ -205,7 +229,22 @@
     ]
     for copy in rims:
         copy.start()
-    scatter(0)
+    keep(0)
+    at_distances(near, functools.partial(send_to, 0))
+    same_plane(functools.partial(send_to, 0))
+    pack(1, filt[:, width : 2 * width])
+    keep(1)
+    at_distances(near, functools.partial(send_to, 1))
+    same_plane(functools.partial(send_to, 1))
+    pl.semaphore_wait(told.at[0], 1)
+    at_distances(far[:1], functools.partial(send_to, 0))
+    at_distances(far[:1], functools.partial(send_to, 1))
+    pl.semaphore_wait(told.at[1], 1)
+    at_distances(far[1:], functools.partial(send_to, 0))
+    at_distances(far[1:], functools.partial(send_to, 1))
+    pl.semaphore_wait(told.at[2], 1)
+    at_distances((4,), functools.partial(send_to, 0))
+    at_distances((4,), functools.partial(send_to, 1))
     for load in loads[4:6]:
         load.wait()
     for copy in rims:
@@ -222,7 +261,7 @@
 
     for q in range(CHUNKS):
         columns = slice(q * width, (q + 1) * width)
-        if q:
+        if q > 1:
             pack(q, filt[:, columns])
             scatter(q)
         gated = short(keys, 0, key_taps, columns) * short(values, 1, value_taps, columns)
@@ -312,6 +351,7 @@
             pltpu.SemaphoreType.DMA((2,)),
             pltpu.SemaphoreType.DMA((3 * CHUNKS,)),
             pltpu.SemaphoreType.DMA((3 * CHUNKS,)),
+            pltpu.SemaphoreType.REGULAR((3,)),
         ],
         compiler_params=pltpu.CompilerParams(
             collective_id=0, has_side_effects=True, vmem_limit_bytes=63 * 1024 * 1024

time: 47.9 us -> 47.7 us (level)
  no operation moved by 1% of the time
where the time goes in v4:
time: 47.7 us; the launch traced here: 47.6 us
  Pallas kernels  46.8 us (98%)
  local copies, waits for them, and re-layouts  0.8 us (2%)
    pallas_call x1, Pallas kernels, on_device(): pl.pallas_call(functools.partial(kernel, n), out_shape=pltpu.VMEM((rows,...  46.8 us

profile of v4, /device:TPU:1, one launch (start us, length us, event | category | flops | bytes accessed | tf_op | source)
XLA Modules:
  0.0 47.6 jit_solution(2019820768313682556)
XLA Ops:
  0.0 46.8 %shard_map.109 = bf16[512,512]{1,0:T(8,128)(2,1)S(1)} custom-call(bf16[512,512]{1,0:T(8,128)(2,1)} %key_hbm.1, bf16[512,512]{1,0:T(8,128)(2,1)} %value_hbm.1, f32[3,512]{1,0:T(4,128)} %key_taps_hbm.1, f32[3,512]{1,0:T(4,128)} %value_taps_hbm.1, bf16[512,512]{1,0:T(8,128)(2,1)} %filter_hbm.1, f32[512]{0:T(512)} %skip_hbm.1, ...), custom_call_target="tpu_custom_call" | custom-call | tf_op jit(solution)/shard_map/pallas_call | solution.py:326
  46.8 0.8 %copy.13 = bf16[512,512]{1,0:T(8,128)(2,1)} copy(bf16[512,512]{1,0:T(8,128)(2,1)S(1)} %shard_map.109) | data formatting | bytes 1048576

commit v5 on v4

--- a/solution.py
+++ b/solution.py
@@ -151,7 +151,7 @@
             )
         )
     ]
-    for load in loads:
+    for load in loads[:7]:
         load.start()
 
     def pack(slot, block):
@@ -232,6 +232,8 @@
     keep(0)
     at_distances(near, functools.partial(send_to, 0))
     same_plane(functools.partial(send_to, 0))
+    for load in loads[7:]:
+        load.start()
     pack(1, filt[:, width : 2 * width])
     keep(1)
     at_distances(near, functools.partial(send_to, 1))

time: 47.7 us -> 47.7 us (level)
  no operation moved by 1% of the time
where the time goes in v5:
time: 47.7 us; the launch traced here: 47.6 us
  Pallas kernels  46.8 us (98%)
  local copies, waits for them, and re-layouts  0.8 us (2%)
    pallas_call x1, Pallas kernels, on_device(): pl.pallas_call(functools.partial(kernel, n), out_shape=pltpu.VMEM((rows,...  46.8 us

profile of v5, /device:TPU:1, one launch (start us, length us, event | category | flops | bytes accessed | tf_op | source)
XLA Modules:
  0.0 47.6 jit_solution(8984227326522588048)
XLA Ops:
  0.0 46.8 %shard_map.109 = bf16[512,512]{1,0:T(8,128)(2,1)S(1)} custom-call(bf16[512,512]{1,0:T(8,128)(2,1)} %key_hbm.1, bf16[512,512]{1,0:T(8,128)(2,1)} %value_hbm.1, f32[3,512]{1,0:T(4,128)} %key_taps_hbm.1, f32[3,512]{1,0:T(4,128)} %value_taps_hbm.1, bf16[512,512]{1,0:T(8,128)(2,1)} %filter_hbm.1, f32[512]{0:T(512)} %skip_hbm.1, ...), custom_call_target="tpu_custom_call" | custom-call | tf_op jit(solution)/shard_map/pallas_call | solution.py:328
  46.8 0.8 %copy.13 = bf16[512,512]{1,0:T(8,128)(2,1)} copy(bf16[512,512]{1,0:T(8,128)(2,1)S(1)} %shard_map.109) | data formatting | bytes 1048576
